TPU v7x, 256 devices: a whole 4x4x8 slice. The times are simulated.
256 devices in a mesh: outer: 16 (over z, x_lo), inner: 16 (over x_hi, y, core).
Axes of the slice: x: 4 (x_hi: 2, x_lo: 2; x = x_hi * 2 + x_lo), y: 4, z: 8, core: 2. Of those that a mesh axis runs over, the one named last changes fastest.
Arguments:
- queries: bfloat16 [32768, 4096], P(('outer', 'inner')), may hold values from -64 to 64
- keys: bfloat16 [32768, 1024], P(('outer', 'inner')), may hold values from -8 to 8
- values: bfloat16 [32768, 1024], P(('outer', 'inner')), may hold values from -6 to 6
- span_order: int32 [512], replicated, may hold values from 0 to 511, as said below
Outputs:
- attended: bfloat16 [32768, 4096], P(('outer', 'inner'))
Inputs may be any that keep to these rules, and one draw needn't show every extreme that they name: span_order is a permutation of 0 .. 511, and the two spans of every device sum to 511.
All inputs are finite; a program needn't handle non-finite values.
Results may differ from a plain program's by a relative error of at most 0.0055.
Values may be sent and summed in bfloat16 or wider, within the bound.
A program may use at most 64 MiB of HBM per device.

v0:
```python
import math

import jax
import jax.numpy as jnp
from jax import lax
from jax.sharding import PartitionSpec as P

QH = 32
KVH = 8
HEAD = 128
GROUP = 4
INNER_STEPS = 3
OUTER_ROUNDS = 2


def from_behind(block, axis, distance):
    devices = range(lax.axis_size(axis))
    route = [((i - distance) % len(devices), i) for i in devices]
    return lax.ppermute(block, axis, route)


def token_positions(span_order, device, span_len):
    offsets = jnp.arange(2 * span_len, dtype=jnp.int32)
    starts = jnp.take(span_order, 2 * device + offsets // span_len)
    return starts * span_len + offsets % span_len


def absorb(state, grouped, query_pos, pair_block, key_pos):
    peak_old, totals, accum = state
    key_heads = pair_block[0].reshape(-1, KVH, HEAD)
    value_heads = pair_block[1].reshape(-1, KVH, HEAD)
    scores = jnp.einsum("tgrd,ugd->tgru", grouped, key_heads, preferred_element_type=jnp.float32)
    scores = scores * (1.0 / math.sqrt(HEAD))
    visible = key_pos[None, :] <= query_pos[:, None]
    scores = jnp.where(visible[:, None, None, :], scores, -jnp.inf)
    peak_new = jnp.maximum(peak_old, jnp.max(scores, axis=-1))
    factor = jnp.exp(peak_old - peak_new)
    weights = jnp.exp(scores - peak_new[..., None])
    totals = totals * factor + jnp.sum(weights, axis=-1)
    update = jnp.einsum(
        "tgru,ugd->tgrd",
        weights.astype(jnp.bfloat16),
        value_heads,
        preferred_element_type=jnp.float32,
    )
    accum = accum * factor[..., None] + update
    return (peak_new, totals, accum)


def on_device(queries, keys, values, span_order):
    row_count = queries.shape[0]
    span_len = row_count // 2
    n_inner = lax.axis_size("inner")
    n_outer = lax.axis_size("outer")
    outer_id = lax.axis_index("outer")
    inner_id = lax.axis_index("inner")
    own_device = outer_id * n_inner + inner_id
    query_pos = token_positions(span_order, own_device, span_len)
    grouped = queries.reshape(row_count, KVH, GROUP, HEAD)
    state = (
        jnp.full((row_count, KVH, GROUP), -jnp.inf, jnp.float32),
        jnp.zeros((row_count, KVH, GROUP), jnp.float32),
        jnp.zeros((row_count, KVH, GROUP, HEAD), jnp.float32),
    )
    own_pair = jnp.stack([keys, values])

    def source_pos(outer_src, rotation):
        source = outer_src * n_inner + (inner_id - rotation) % n_inner
        return token_positions(span_order, source, span_len)

    base_pair = own_pair
    for rounds in range(OUTER_ROUNDS):
        if rounds > 0:
            base_pair = from_behind(base_pair, "outer", 1)
        outer_src = (outer_id - rounds) % n_outer
        inner_state = state
        current = base_pair
        collected = [base_pair]
        inner_state = absorb(inner_state, grouped, query_pos, base_pair, source_pos(outer_src, 0))
        for inner_rotation in range(1, INNER_STEPS + 1):
            current = from_behind(current, "inner", 1)
            collected.append(current)
            inner_state = absorb(
                inner_state, grouped, query_pos, current, source_pos(outer_src, inner_rotation)
            )
        state = inner_state
    peak_final, totals, accum = state
    blended = accum / totals[..., None]
    return blended.reshape(row_count, QH * HEAD).astype(jnp.bfloat16)


def solution(mesh):
    placed = (
        P(("outer", "inner"), None),
        P(("outer", "inner"), None),
        P(("outer", "inner"), None),
        P(),
    )
    return jax.shard_map(
        on_device,
        mesh=mesh,
        in_specs=placed,
        out_specs=P(("outer", "inner"), None),
        check_vma=False,
    )
```

profile of v0, /device:TPU:6, one launch (start us, length us, event | category | flops | bytes accessed | tf_op | source)
XLA Modules:
  0.0 81.1 jit_solution(17011172948549355271)
XLA Ops:
  0.0 1.1 %copy.85 = bf16[128,1024]{0,1:T(8,128)(2,1)S(1)} copy(bf16[128,1024]{1,0:T(8,128)(2,1)} %param.8) | data formatting | bytes 524288 | tf_op jit(solution)/shard_map/reshape;squeeze;stack | solution.py:31
  1.1 1.1 %copy.35 = bf16[128,1024]{0,1:T(8,128)(2,1)S(1)} copy(bf16[128,1024]{1,0:T(8,128)(2,1)} %param.7) | data formatting | bytes 524288 | tf_op args[1]
  2.3 0.8 %pad_maximum_fusion = bf16[2,128,1024]{1,2,0:T(8,128)(2,1)} fusion(bf16[1,128,1024]{1,2,0:T(8,128)(2,1)S(1)} %bitcast.177, bf16[1,128,1024]{1,2,0:T(8,128)(2,1)S(1)} %bitcast.187), kind=kLoop, calls=%fused_computation.73 | loop fusion | flops 262144 | bytes 1048576 | tf_op jit(solution)/shard_map/stack | solution.py:65
  3.1 2.2 %collective-permute-start.3 = (bf16[2,128,1024]{1,2,0:T(8,128)(2,1)}, bf16[2,128,1024]{1,2,0:T(8,128)(2,1)S(1)}, u32[]{:S(2)}, u32[]{:S(2)}) collective-permute-start(bf16[2,128,1024]{1,2,0:T(8,128)(2,1)} %pad_maximum_fusion), channel_id=1, source_target_pairs={{240,0},{0,16},{16,32},{32,48},{48,64},{64,80},{80,96},{96,112},{1... | collective-permute-start | bytes 1572872 | tf_op jit(solution)/shard_map/ppermute | solution.py:19
  5.5 1.3 %gather_fusion.8 = s32[128]{0:T(128)S(1)} fusion(s32[512]{0:T(512)S(1)} %copy-done, s32[1024]{0:T(1024)S(1)} %pad_clamp_fusion), kind=kCustom, calls=%fused_computation.8.clone | custom fusion | bytes 1536 | tf_op jit(solution)/shard_map/jit(_take)/gather | solution.py:24
  6.7 1.3 %gather_fusion.7 = s32[128]{0:T(128)S(1)} fusion(s32[512]{0:T(512)S(1)} %copy-done, s32[1024]{0:T(1024)S(1)} %pad_clamp_fusion.1), kind=kCustom, calls=%fused_computation.7.clone | custom fusion | bytes 1536 | tf_op jit(solution)/shard_map/jit(_take)/gather | solution.py:24
  8.0 1.3 %gather_fusion.6 = s32[128]{0:T(128)S(1)} fusion(s32[512]{0:T(512)S(1)} %copy-done, s32[1024]{0:T(1024)S(1)} %pad_clamp_fusion.2), kind=kCustom, calls=%fused_computation.6.clone | custom fusion | bytes 1536 | tf_op jit(solution)/shard_map/jit(_take)/gather | solution.py:24
  9.3 1.3 %gather_fusion.5 = s32[128]{0:T(128)S(1)} fusion(s32[512]{0:T(512)S(1)} %copy-done, s32[1024]{0:T(1024)S(1)} %pad_clamp_fusion.3), kind=kCustom, calls=%fused_computation.5.clone | custom fusion | bytes 1536 | tf_op jit(solution)/shard_map/jit(_take)/gather | solution.py:24
  10.6 1.3 %gather_fusion.1 = s32[128]{0:T(128)S(1)} fusion(s32[512]{0:T(512)S(1)} %copy-done, s32[1024]{0:T(1024)S(1)} %pad_clamp_fusion.7), kind=kCustom, calls=%fused_computation.1.clone | custom fusion | bytes 1536 | tf_op jit(solution)/shard_map/jit(_take)/gather | solution.py:24
  11.9 1.3 %gather_fusion.4 = s32[128]{0:T(128)S(1)} fusion(s32[512]{0:T(512)S(1)} %copy-done, s32[1024]{0:T(1024)S(1)} %pad_clamp_fusion.4), kind=kCustom, calls=%fused_computation.4.clone | custom fusion | bytes 1536 | tf_op jit(solution)/shard_map/jit(_take)/gather | solution.py:24
  13.2 1.3 %gather_fusion.3 = s32[128]{0:T(128)S(1)} fusion(s32[512]{0:T(512)S(1)} %copy-done, s32[1024]{0:T(1024)S(1)} %pad_clamp_fusion.5), kind=kCustom, calls=%fused_computation.3.clone | custom fusion | bytes 1536 | tf_op jit(solution)/shard_map/jit(_take)/gather | solution.py:24
  14.5 1.3 %gather_fusion.2 = s32[128]{0:T(128)S(1)} fusion(s32[512]{0:T(512)S(1)} %copy-done, s32[1024]{0:T(1024)S(1)} %pad_clamp_fusion.6), kind=kCustom, calls=%fused_computation.2.clone | custom fusion | bytes 1536 | tf_op jit(solution)/shard_map/jit(_take)/gather | solution.py:24
  15.8 1.3 %gather_fusion = s32[128]{0:T(128)S(1)} fusion(s32[512]{0:T(512)S(1)} %copy-done, s32[1024]{0:T(1024)S(1)} %pad_clamp_fusion.8), kind=kCustom, calls=%fused_computation.clone | custom fusion | bytes 1536 | tf_op jit(solution)/shard_map/jit(_take)/gather | solution.py:24
  17.1 0.8 reshape.394
  18.2 0.7 fusion.71
  19.7 9.4 %collective-permute-done = bf16[2,128,1024]{1,2,0:T(8,128)(2,1)} collective-permute-done((bf16[2,128,1024]{1,2,0:T(8,128)(2,1)}, bf16[2,128,1024]{1,2,0:T(8,128)(2,1)}, u32[]{:S(2)}, u32[]{:S(2)}) %collective-permute-start) | collective-permute-done | bytes 524320 | tf_op jit(solution)/shard_map/ppermute | solution.py:19
  29.1 1.1 %fusion.59 = (bf16[1,128,1024]{1,2,0:T(8,128)(2,1)S(1)}, bf16[1,128,1024]{1,2,0:T(8,128)(2,1)S(1)}) fusion(bf16[2,128,1024]{1,2,0:T(8,128)(2,1)} %collective-permute-done), kind=kLoop, calls=%fused_computation.143 | loop fusion | bytes 1048576 | tf_op jit(solution)/shard_map/slice | solution.py:31
  30.2 0.7 fusion.72
  31.0 0.7 fusion.68
  31.6 9.9 %collective-permute-done.1 = bf16[2,128,1024]{1,2,0:T(8,128)(2,1)S(1)} collective-permute-done((bf16[2,128,1024]{1,2,0:T(8,128)(2,1)}, bf16[2,128,1024]{1,2,0:T(8,128)(2,1)S(1)}, u32[]{:S(2)}, u32[]{:S(2)}) %collective-permute-start.1) | collective-permute-done | bytes 524320 | tf_op jit(solution)/shard_map/ppermute | solution.py:19
  41.6 0.7 fusion.70
  42.2 4.9 %collective-permute-done.4 = bf16[2,128,1024]{1,2,0:T(8,128)(2,1)S(1)} collective-permute-done((bf16[2,128,1024]{1,2,0:T(8,128)(2,1)S(1)}, bf16[2,128,1024]{1,2,0:T(8,128)(2,1)S(1)}, u32[]{:S(2)}, u32[]{:S(2)}) %collective-permute-start.4) | collective-permute-done | bytes 524320 | tf_op jit(solution)/shard_map/ppermute | solution.py:19
  47.2 0.7 fusion.67
  47.8 5.9 %collective-permute-done.2 = bf16[2,128,1024]{1,2,0:T(8,128)(2,1)S(1)} collective-permute-done((bf16[2,128,1024]{1,2,0:T(8,128)(2,1)S(1)}, bf16[2,128,1024]{1,2,0:T(8,128)(2,1)S(1)}, u32[]{:S(2)}, u32[]{:S(2)}) %collective-permute-start.2) | collective-permute-done | bytes 524320 | tf_op jit(solution)/shard_map/ppermute | solution.py:19
  53.8 0.7 fusion.69
  54.4 4.9 %collective-permute-done.5 = bf16[2,128,1024]{1,2,0:T(8,128)(2,1)S(1)} collective-permute-done((bf16[2,128,1024]{1,2,0:T(8,128)(2,1)S(1)}, bf16[2,128,1024]{1,2,0:T(8,128)(2,1)S(1)}, u32[]{:S(2)}, u32[]{:S(2)}) %collective-permute-start.5) | collective-permute-done | bytes 524320 | tf_op jit(solution)/shard_map/ppermute | solution.py:19
  59.4 0.7 fusion.66
  60.1 11.5 %collective-permute-done.6 = bf16[2,128,1024]{1,2,0:T(8,128)(2,1)S(1)} collective-permute-done((bf16[2,128,1024]{1,2,0:T(8,128)(2,1)S(1)}, bf16[2,128,1024]{1,2,0:T(8,128)(2,1)S(1)}, u32[]{:S(2)}, u32[]{:S(2)}) %collective-permute-start.6) | collective-permute-done | bytes 524320 | tf_op jit(solution)/shard_map/ppermute | solution.py:19
  71.6 0.7 fusion.65
  73.6 0.5 fusion.36
  78.0 1.8 %fusion.1 = bf16[128,8,4,128]{0,3,2,1:T(8,128)(2,1)S(1)} fusion(f32[8,128,128,4]{2,1,3,0:T(8,128)S(1)} %fusion.26, f32[8,128,128,4]{2,1,3,0:T(8,128)S(1)} %fusion.28, f32[8,128,128,4]{2,1,3,0:T(8,128)S(1)} %fusion.30, f32[8,128,128,4]{2,1,3,0:T(8,128)S(1)} %fusion.32, f32[8,128,128,4]{2,1,3,0:T(8,128)S(1)} %fusion.34, f32[8,128,128,4]{2,1,3,0:T(8,128)S(1)} %fusion.36, ...), kind=kOutput, calls=%fused_computation.11 | convolution fusion | flops 144179200 | bytes 18251776 | tf_op jit(solution)/shard_map/tgru,ugd->tgrd/dot_general | solution.py:40
  79.8 1.3 %copy.58 = bf16[128,4096]{1,0:T(8,128)(2,1)} copy(bf16[128,4096]{0,1:T(8,128)(2,1)S(1)} %bitcast.176) | data formatting | bytes 2097152 | tf_op jit(solution)/shard_map/convert_element_type | solution.py:89
  (60 shorter events, 6.8 us)
Async XLA Ops:
  0.0 5.5 %copy-start = (s32[512]{0:T(512)S(1)}, s32[512]{0:T(512)}, u32[]{:S(2)}) copy-start(s32[512]{0:T(512)} %param.9) | copy-start | bytes 6148
  3.1 27.7 %collective-permute-start.3 = (bf16[2,128,1024]{1,2,0:T(8,128)(2,1)}, bf16[2,128,1024]{1,2,0:T(8,128)(2,1)S(1)}, u32[]{:S(2)}, u32[]{:S(2)}) collective-permute-start(bf16[2,128,1024]{1,2,0:T(8,128)(2,1)} %pad_maximum_fusion), channel_id=1, source_target_pairs={{240,0},{0,16},{16,32},{32,48},{48,64},{64,80},{80,96},{96,112},{1... | collective-permute-start | bytes 1572872 | tf_op jit(solution)/shard_map/ppermute | solution.py:19
  5.3 23.8 %collective-permute-start = (bf16[2,128,1024]{1,2,0:T(8,128)(2,1)}, bf16[2,128,1024]{1,2,0:T(8,128)(2,1)}, u32[]{:S(2)}, u32[]{:S(2)}) collective-permute-start(bf16[2,128,1024]{1,2,0:T(8,128)(2,1)} %pad_maximum_fusion), channel_id=1, source_target_pairs={{15,0},{0,1},{1,2},{2,3},{3,4},{4,5},{5,6},{6,7},{7,8},{8,9},{9,10... | collective-permute-start | bytes 1572872 | tf_op jit(solution)/shard_map/ppermute | solution.py:19
  6.7 10.3 %copy-start.2 = (bf16[128,1024]{1,0:T(8,128)(2,1)S(1)}, bf16[128,1024]{1,0:T(8,128)(2,1)}, u32[]{:S(2)}) copy-start(bf16[128,1024]{1,0:T(8,128)(2,1)} %param.7) | copy-start | bytes 786436
  8.0 9.1 %copy-start.1 = (bf16[128,4096]{1,0:T(8,128)(2,1)S(1)}, bf16[128,4096]{1,0:T(8,128)(2,1)}, u32[]{:S(2)}) copy-start(bf16[128,4096]{1,0:T(8,128)(2,1)} %param.6) | copy-start | bytes 3145732
  29.1 12.4 %collective-permute-start.1 = (bf16[2,128,1024]{1,2,0:T(8,128)(2,1)}, bf16[2,128,1024]{1,2,0:T(8,128)(2,1)S(1)}, u32[]{:S(2)}, u32[]{:S(2)}) collective-permute-start(bf16[2,128,1024]{1,2,0:T(8,128)(2,1)} %collective-permute-done), channel_id=1, source_target_pairs={{15,0},{0,1},{1,2},{2,3},{3,4},{4,5},{5,6},{6,7},{7,8},{8,9},{9,10... | collective-permute-start | bytes 1572872 | tf_op jit(solution)/shard_map/ppermute | solution.py:19
  30.8 16.3 %collective-permute-start.4 = (bf16[2,128,1024]{1,2,0:T(8,128)(2,1)S(1)}, bf16[2,128,1024]{1,2,0:T(8,128)(2,1)S(1)}, u32[]{:S(2)}, u32[]{:S(2)}) collective-permute-start(bf16[2,128,1024]{1,2,0:T(8,128)(2,1)S(1)} %collective-permute-done.3), channel_id=1, source_target_pairs={{15,0},{0,1},{1,2},{2,3},{3,4},{4,5},{5,6},{6,7},{7,8},{8,9},{9,10... | collective-permute-start | bytes 1572872 | tf_op jit(solution)/shard_map/ppermute | solution.py:19
  41.5 12.2 %collective-permute-start.2 = (bf16[2,128,1024]{1,2,0:T(8,128)(2,1)S(1)}, bf16[2,128,1024]{1,2,0:T(8,128)(2,1)S(1)}, u32[]{:S(2)}, u32[]{:S(2)}) collective-permute-start(bf16[2,128,1024]{1,2,0:T(8,128)(2,1)S(1)} %collective-permute-done.1), channel_id=1, source_target_pairs={{15,0},{0,1},{1,2},{2,3},{3,4},{4,5},{5,6},{6,7},{7,8},{8,9},{9,10... | collective-permute-start | bytes 1572872 | tf_op jit(solution)/shard_map/ppermute | solution.py:19
  47.1 12.2 %collective-permute-start.5 = (bf16[2,128,1024]{1,2,0:T(8,128)(2,1)S(1)}, bf16[2,128,1024]{1,2,0:T(8,128)(2,1)S(1)}, u32[]{:S(2)}, u32[]{:S(2)}) collective-permute-start(bf16[2,128,1024]{1,2,0:T(8,128)(2,1)S(1)} %collective-permute-done.4), channel_id=1, source_target_pairs={{15,0},{0,1},{1,2},{2,3},{3,4},{4,5},{5,6},{6,7},{7,8},{8,9},{9,10... | collective-permute-start | bytes 1572872 | tf_op jit(solution)/shard_map/ppermute | solution.py:19
  59.4 12.2 %collective-permute-start.6 = (bf16[2,128,1024]{1,2,0:T(8,128)(2,1)S(1)}, bf16[2,128,1024]{1,2,0:T(8,128)(2,1)S(1)}, u32[]{:S(2)}, u32[]{:S(2)}) collective-permute-start(bf16[2,128,1024]{1,2,0:T(8,128)(2,1)S(1)} %collective-permute-done.5), channel_id=1, source_target_pairs={{15,0},{0,1},{1,2},{2,3},{3,4},{4,5},{5,6},{6,7},{7,8},{8,9},{9,10... | collective-permute-start | bytes 1572872 | tf_op jit(solution)/shard_map/ppermute | solution.py:19
where the time goes:
time: 81.2 us; the launch traced here: 81.1 us
  waiting for transfers between devices  46.5 us (57%)
  local copies, waits for them, and re-layouts  17.1 us (21%)
  matrix products  10.4 us (13%)
  other arithmetic  4.53 us (6%)
  starting transfers between devices  2.28 us (3%)
    ppermute x7, waiting for transfers between devices, from_behind(): return lax.ppermute(block, axis, route)  46.5 us
    gather x9, local copies, waits for them, and re-layouts, token_positions(): starts = jnp.take(span_order, 2 * device + offsets // span_len)  11.4 us
    dot_general x8, matrix products, absorb(): jnp.einsum('tgrd,ugd->tgru', grouped, key_heads, preferred_element_type=j...  5.35 us
    dot_general x8, matrix products, absorb(): jnp.einsum('tgru,ugd->tgrd', weights.astype(jnp.bfloat16), value_heads, p...  5 us
    reduce_sum x8, other arithmetic, absorb(): totals = totals * factor + jnp.sum(weights, axis=-1)  3.23 us
    ppermute x7, starting transfers between devices, from_behind(): return lax.ppermute(block, axis, route)  2.28 us
  transfers between devices with their start and end apart: 7, of which 6 were waited for; matrix products, arithmetic and copies ran while one was open for 24% of the time, Pallas kernels for 0%

commit v1 on v0

v1 whole, which is shorter than its diff:
```python
import functools
import math

import jax
import jax.numpy as jnp
from jax import lax
from jax.experimental import pallas as pl
from jax.experimental.pallas import tpu as pltpu
from jax.sharding import PartitionSpec as P

ROLES = 6
BLOCKS = 2
HEADS = 4
GROUP = 4
HEAD = 128
QUARTER = GROUP * HEAD
MESH = pl.DeviceIdType.MESH
MASKED = -1e30

OFFSETS = ((-1, 1), (-1, 2), (0, -1), (0, 1), (0, 2), (1, -1), (1, 0), (1, 1), (1, 2))

ORDER = (3, 2, 1, 5, 4)

ROUTES = {
    (0, 0, 1): (0xFF3F, 0x7F3F, 0x3F3F, 0x3F3F),
    (0, 0, 3): (0xFFFF, 0xFFFF, 0xFFFF, 0xFFFF),
    (0, 0, 4): (0x00C0, 0x80C0, 0xC0C0, 0xC8CB),
    (0, 1, 1): (0x3030, 0x3030, 0x3000, 0x1000),
    (0, 1, 2): (0xFF0F, 0xFF8F, 0xCFFF, 0xEFFF),
    (0, 1, 3): (0xFFFF, 0xFFFF, 0xFFFF, 0xFFFF),
    (0, 1, 4): (0x0000, 0x0080, 0x0000, 0x0000),
    (0, 1, 5): (0x00F0, 0x8070, 0xF800, 0xDC8C),
    (1, 0, 4): (0xCFDC, 0x05C4, 0x00C0, 0x0000),
    (2, 1, 1): (0xFCF0, 0xFCF8, 0xFCFF, 0xFEFF),
    (2, 1, 4): (0x0F00, 0x0700, 0x000F, 0x0207),
    (2, 1, 5): (0x3F30, 0x3738, 0x30FF, 0x3237),
    (3, 0, 1): (0xC000, 0xC080, 0xC0C0, 0xC0C0),
    (3, 0, 4): (0x080C, 0x0E3E, 0x0F3F, 0x3437),
    (3, 1, 1): (0xC000, 0x4000, 0x0000, 0x0000),
    (3, 1, 2): (0xF000, 0x7000, 0x0030, 0x0010),
    (3, 1, 4): (0x0F0F, 0x0F0F, 0x0F07, 0x0303),
    (3, 1, 5): (0x0C0C, 0x0C0C, 0x0004, 0x0000),
    (5, 1, 4): (0x0F00, 0x0708, 0x008F, 0xC8CD),
}

SEEN = {
    0: ((0,), (0, 1)),
    1: ((0, 1), (0, 1)),
    2: ((1,), ()),
    3: ((0,), (0, 1)),
    4: ((0, 1), (0, 1)),
    5: ((1,), ()),
}


def needed(role):
    return sorted(set(SEEN[role][0]) | set(SEEN[role][1]))


def kernel(order_ref, q_ref, k_ref, v_ref, o_ref, held, qbuf, obuf, peak, total, acc, hidden,
           send_sem, recv_sem, swap_sem, q_sem, qswap_sem, o_sem):
    n_outer = lax.axis_size("outer")
    n_chips = lax.axis_size("inner") // 2
    outer = lax.axis_index("outer")
    inner = lax.axis_index("inner")
    chip, core = inner // 2, inner % 2
    kind = ((outer % 2) * 4 + chip % 4) * 2 + core
    other = 1 - core

    def device(d_outer, d_chip):
        return (
            lax.rem(outer + d_outer + n_outer, n_outer),
            lax.rem(chip + d_chip + n_chips, n_chips) * 2 + core,
        )

    twin = (outer, chip * 2 + other)

    barrier = pltpu.get_barrier_semaphore()
    for d_outer, d_chip in OFFSETS:
        pl.semaphore_signal(barrier, 1, device_id=device(-d_outer, -d_chip), device_id_type=MESH)
    pl.semaphore_signal(barrier, 1, device_id=twin, device_id_type=MESH)

    def own_copy(ref, part, head):
        columns = pl.ds((core * HEADS + head) * HEAD, HEAD)
        return pltpu.make_async_copy(
            ref.at[:, columns], held.at[0, core, head, part], recv_sem.at[0, core, head]
        )

    def twin_copy(ref, part, head):
        columns = pl.ds((other * HEADS + head) * HEAD, HEAD)
        return pltpu.make_async_remote_copy(
            src_ref=ref.at[:, columns],
            dst_ref=held.at[0, core, head, part],
            send_sem=swap_sem.at[head, part],
            recv_sem=recv_sem.at[0, core, head],
            device_id=twin,
            device_id_type=MESH,
        )

    width = HEADS * QUARTER

    def own_queries():
        return pltpu.make_async_copy(
            q_ref.at[:, pl.ds(core * width, width)], qbuf.at[core], q_sem.at[core]
        )

    def twin_queries():
        return pltpu.make_async_remote_copy(
            src_ref=q_ref.at[:, pl.ds(other * width, width)],
            dst_ref=qbuf.at[core],
            send_sem=qswap_sem,
            recv_sem=q_sem.at[core],
            device_id=twin,
            device_id_type=MESH,
        )

    for head in range(HEADS):
        for part, ref in enumerate((k_ref, v_ref)):
            own_copy(ref, part, head).start()
    own_queries().start()

    def hidden_tile(role, query_core, key_core):
        d_outer, d_chip = role // 3, role % 3
        at_outer, at_inner = device(-d_outer, -d_chip)
        source = at_outer * (2 * n_chips) + (at_inner - core) + key_core
        mine = outer * (2 * n_chips) + chip * 2 + query_core
        row = lax.broadcasted_iota(jnp.int32, (HEAD, HEAD), 0)
        column = lax.broadcasted_iota(jnp.int32, (HEAD, HEAD), 1)
        half = HEAD // 2
        row_at = jnp.where(row < half, order_ref[2 * mine] * half, order_ref[2 * mine + 1] * half - half) + row
        column_at = (
            jnp.where(column < half, order_ref[2 * source] * half, order_ref[2 * source + 1] * half - half) + column
        )
        return jnp.where(column_at <= row_at, 0.0, MASKED)

    def pass_on(role, block, head, unit):
        for there in range(1, ROLES):
            masks = ROUTES.get((role, block, there))
            if masks is None:
                continue
            mask = jnp.int32(masks[0])
            for at in range(1, HEADS):
                mask = jnp.where(head == at, jnp.int32(masks[at]), mask)
            copy = pltpu.make_async_remote_copy(
                src_ref=held.at[role, block, head],
                dst_ref=held.at[there, block, head],
                send_sem=send_sem.at[role, block, head, there - 1],
                recv_sem=recv_sem.at[there, block, head],
                device_id=device(there // 3 - role // 3, there % 3 - role % 3),
                device_id_type=MESH,
            )

            @pl.when(lax.rem(lax.shift_right_logical(mask, kind), 2) == 1)
            def _():
                unit(copy)

    def arrive(role, block, head):
        chunk = held.at[role, block, head]
        pltpu.make_async_copy(chunk, chunk, recv_sem.at[role, block, head]).wait()

    def start(copy):
        copy.start()

    def finish(copy):
        copy.wait_send()

    pl.semaphore_wait(barrier, len(OFFSETS) + 1)

    for head in range(HEADS):
        for part, ref in enumerate((k_ref, v_ref)):
            twin_copy(ref, part, head).start()

    @pl.loop(0, HEADS)
    def _(head):
        arrive(0, core, head)
        for block in range(BLOCKS):
            @pl.when(core == block)
            def _():
                pass_on(0, block, head, start)

    twin_queries().start()

    @pl.loop(0, HEADS)
    def _(head):
        arrive(0, other, head)
        for block in range(BLOCKS):
            @pl.when(other == block)
            def _():
                pass_on(0, block, head, start)

    for role in range(ROLES):
        for query_core in range(2):
            for key_core in SEEN[role][query_core]:
                hidden[role, query_core, key_core] = hidden_tile(role, query_core, key_core)

    scale = math.log2(math.e) / math.sqrt(HEAD)

    def attend(role, head):
        for query_core in range(2):
            seen = SEEN[role][query_core]
            if not seen:
                continue
            queries = jnp.concatenate(
                [
                    qbuf[query_core, :, pl.ds(pl.multiple_of((head * GROUP + at) * HEAD, HEAD), HEAD)]
                    for at in range(GROUP)
                ],
                axis=0,
            )
            scores = []
            for key_core in seen:
                score = lax.dot_general(
                    queries,
                    held[role, key_core, head, 0],
                    (((1,), (1,)), ((), ())),
                    preferred_element_type=jnp.float32,
                )
                cover = hidden[role, query_core, key_core]
                score = score.reshape(GROUP, HEAD, HEAD) * scale + cover[None]
                scores.append(score.reshape(QUARTER, HEAD))
            top = scores[0] if len(seen) == 1 else jnp.maximum(scores[0], scores[1])
            top = jnp.max(top, axis=1, keepdims=True)
            if role == 0:
                new = jnp.broadcast_to(top, (QUARTER, HEAD))
            else:
                old = peak[query_core, head]
                new = jnp.maximum(old, top)
                factor = jnp.exp2(old - new)
            weights = [jnp.exp2(score - new) for score in scores]
            summed = weights[0] if len(seen) == 1 else weights[0] + weights[1]
            update = None
            for key_core, weight in zip(seen, weights):
                term = jnp.dot(
                    weight.astype(jnp.bfloat16),
                    held[role, key_core, head, 1],
                    preferred_element_type=jnp.float32,
                )
                update = term if update is None else update + term
            peak[query_core, head] = new
            if role == 0:
                total[query_core, head] = summed
                acc[query_core, head] = update
            else:
                total[query_core, head] = total[query_core, head] * factor + summed
                acc[query_core, head] = acc[query_core, head] * factor + update

    for query_core in range(2):
        pltpu.make_async_copy(qbuf.at[query_core], qbuf.at[query_core], q_sem.at[query_core]).wait()

    @pl.loop(0, HEADS)
    def _(head):
        attend(0, head)

    for role in ORDER:
        @pl.loop(0, HEADS)
        def _(head):
            for block in needed(role):
                arrive(role, block, head)
                pass_on(role, block, head, start)
            attend(role, head)

    def own_result(head):
        columns = pl.ds((core * HEADS + head) * QUARTER, QUARTER)
        return pltpu.make_async_copy(obuf.at[core, head], o_ref.at[:, columns], o_sem.at[0, head])

    def twin_result(head):
        columns = pl.ds((core * HEADS + head) * QUARTER, QUARTER)
        return pltpu.make_async_remote_copy(
            src_ref=obuf.at[other, head],
            dst_ref=o_ref.at[:, columns],
            send_sem=o_sem.at[1, head],
            recv_sem=o_sem.at[2, head],
            device_id=twin,
            device_id_type=MESH,
        )

    @pl.loop(0, HEADS)
    def _(head):
        for query_core in range(2):
            sums = jnp.sum(total[query_core, head], axis=1, keepdims=True)
            result = (acc[query_core, head] / sums).astype(jnp.bfloat16)
            for at in range(GROUP):
                obuf[query_core, head, :, at * HEAD : (at + 1) * HEAD] = result[at * HEAD : (at + 1) * HEAD]
        twin_result(head).start()
        own_result(head).start()

    for head in range(HEADS):
        for part, ref in enumerate((k_ref, v_ref)):
            twin_copy(ref, part, head).wait_send()
    twin_queries().wait_send()

    @pl.loop(0, HEADS)
    def _(head):
        for role in range(ROLES):
            for block in needed(role):
                pass_on(role, block, head, finish)
        own_result(head).wait()
        twin_result(head).wait()


def on_device(queries, keys, values, span_order):
    rows = queries.shape[0]
    return pl.pallas_call(
        kernel,
        out_shape=jax.ShapeDtypeStruct(queries.shape, jnp.bfloat16),
        in_specs=[pl.BlockSpec(memory_space=pltpu.SMEM)] + [pl.BlockSpec(memory_space=pl.ANY)] * 3,
        out_specs=pl.BlockSpec(memory_space=pl.ANY),
        scratch_shapes=[
            pltpu.VMEM((ROLES, BLOCKS, HEADS, 2, rows, HEAD), jnp.bfloat16),
            pltpu.VMEM((2, rows, HEADS * QUARTER), jnp.bfloat16),
            pltpu.VMEM((2, HEADS, rows, QUARTER), jnp.bfloat16),
            pltpu.VMEM((2, HEADS, QUARTER, HEAD), jnp.float32),
            pltpu.VMEM((2, HEADS, QUARTER, HEAD), jnp.float32),
            pltpu.VMEM((2, HEADS, QUARTER, HEAD), jnp.float32),
            pltpu.VMEM((ROLES, 2, 2, rows, HEAD), jnp.float32),
            pltpu.SemaphoreType.DMA((ROLES, BLOCKS, HEADS, ROLES - 1)),
            pltpu.SemaphoreType.DMA((ROLES, BLOCKS, HEADS)),
            pltpu.SemaphoreType.DMA((HEADS, 2)),
            pltpu.SemaphoreType.DMA((2,)),
            pltpu.SemaphoreType.DMA,
            pltpu.SemaphoreType.DMA((3, HEADS)),
        ],
        compiler_params=pltpu.CompilerParams(
            collective_id=0, has_side_effects=True, vmem_limit_bytes=48 * 2**20
        ),
        name="attend_window",
    )(span_order, queries, keys, values)


def solution(mesh):
    rows = P(("outer", "inner"), None)
    return jax.shard_map(
        on_device,
        mesh=mesh,
        in_specs=(rows, rows, rows, P()),
        out_specs=rows,
        check_vma=False,
    )
```

time: 81.2 us -> 58 us (0.71)
  the two profiles are of different devices: /device:TPU:6 before, /device:TPU:25 now
where the time goes in v1:
time: 58 us; the launch traced here: 57.8 us
  Pallas kernels  53 us (91%)
  local copies, waits for them, and re-layouts  4.78 us (8%)
    pallas_call x1, Pallas kernels, on_device(): pl.pallas_call(kernel, out_shape=jax.ShapeDtypeStruct(queries.shape, jnp....  53 us
    unnamed x9, local copies, waits for them, and re-layouts  4.78 us

profile of v1, /device:TPU:25, one launch (start us, length us, event | category | flops | bytes accessed | tf_op | source)
XLA Modules:
  0.0 57.8 jit_solution(7339742059418857338)
XLA Ops:
  0.0 0.0 copy-start
  0.0 1.2 %copy-done = bf16[128,4096]{1,0:T(8,128)(2,1)S(1)} copy-done((bf16[128,4096]{1,0:T(8,128)(2,1)S(1)}, bf16[128,4096]{1,0:T(8,128)(2,1)}, u32[]{:S(2)}) %copy-start) | copy-done | bytes 1048600
  1.2 0.0 copy-start.1
  1.2 0.9 %copy-done.1 = bf16[128,1024]{1,0:T(8,128)(2,1)S(1)} copy-done((bf16[128,1024]{1,0:T(8,128)(2,1)S(1)}, bf16[128,1024]{1,0:T(8,128)(2,1)}, u32[]{:S(2)}) %copy-start.1) | copy-done | bytes 262168
  2.2 0.0 copy-start.2
  2.2 0.9 %copy-done.2 = bf16[128,1024]{1,0:T(8,128)(2,1)S(1)} copy-done((bf16[128,1024]{1,0:T(8,128)(2,1)S(1)}, bf16[128,1024]{1,0:T(8,128)(2,1)}, u32[]{:S(2)}) %copy-start.2) | copy-done | bytes 262168
  3.1 0.0 copy-start.3
  3.1 0.7 %copy-done.3 = s32[512]{0:T(512)S(1)} copy-done((s32[512]{0:T(512)S(1)}, s32[512]{0:T(512)}, u32[]{:S(2)}) %copy-start.3) | copy-done | bytes 2072
  3.8 53.0 %attend_window.1 = bf16[128,4096]{1,0:T(8,128)(2,1)S(1)} custom-call(s32[512]{0:T(512)S(1)} %copy-done.3, bf16[128,4096]{1,0:T(8,128)(2,1)S(1)} %copy-done, bf16[128,1024]{1,0:T(8,128)(2,1)S(1)} %copy-done.1, bf16[128,1024]{1,0:T(8,128)(2,1)S(1)} %copy-done.2), custom_call_target="tpu_custom_call" | custom-call | tf_op jit(solution)/shard_map/attend_window/pallas_call | solution.py:303
  56.8 1.0 %copy.6 = bf16[128,4096]{1,0:T(8,128)(2,1)} copy(bf16[128,4096]{1,0:T(8,128)(2,1)S(1)} %attend_window.1) | data formatting | bytes 2097152
Async XLA Ops:
  0.0 1.2 %copy-start = (bf16[128,4096]{1,0:T(8,128)(2,1)S(1)}, bf16[128,4096]{1,0:T(8,128)(2,1)}, u32[]{:S(2)}) copy-start(bf16[128,4096]{1,0:T(8,128)(2,1)} %q_ref.1) | copy-start | bytes 3145732
  1.2 0.9 %copy-start.1 = (bf16[128,1024]{1,0:T(8,128)(2,1)S(1)}, bf16[128,1024]{1,0:T(8,128)(2,1)}, u32[]{:S(2)}) copy-start(bf16[128,1024]{1,0:T(8,128)(2,1)} %k_ref.1) | copy-start | bytes 786436
  2.2 0.9 %copy-start.2 = (bf16[128,1024]{1,0:T(8,128)(2,1)S(1)}, bf16[128,1024]{1,0:T(8,128)(2,1)}, u32[]{:S(2)}) copy-start(bf16[128,1024]{1,0:T(8,128)(2,1)} %v_ref.1) | copy-start | bytes 786436
  3.1 0.7 %copy-start.3 = (s32[512]{0:T(512)S(1)}, s32[512]{0:T(512)}, u32[]{:S(2)}) copy-start(s32[512]{0:T(512)} %order_ref.1) | copy-start | bytes 6148

commit v2 on v1

v2 whole, which is shorter than its diff:
```python
import functools
import math

import jax
import jax.numpy as jnp
from jax import lax
from jax.experimental import pallas as pl
from jax.experimental.pallas import tpu as pltpu
from jax.sharding import PartitionSpec as P

ROLES = 6
BLOCKS = 2
HEADS = 4
GROUP = 4
HEAD = 128
QUARTER = GROUP * HEAD
MESH = pl.DeviceIdType.MESH
MASKED = -1e30

OFFSETS = ((-1, 0), (-1, 1), (-1, 2), (0, -2), (0, -1), (0, 1), (0, 2), (1, -1), (1, 0), (1, 1), (1, 2),)

WIDE = 2
PIECES = HEADS // WIDE

STEPS = (
    (0x403, 0x114, 0x413, 0x301, 0x349, 0xC, 0x1595C, 0x311, 0x15A59, 0x44, 0x4B, 0x4A, 0x25D, 0x5B, 0xDA, 0xCD,),
    (0x11A09, 0x2C5A, 0x104, 0x15A19, 0x441, 0x3, 0x44B, 0x4C, 0x51, 0x1B, 0x4A, 0x1C, 0x53, 0x54, 0xDD, 0xCD,),
    (0x301, 0x411, 0x16259, 0x11A4D, 0x1B, 0x2249, 0x30C, 0x144, 0xB, 0x14, 0x2B5C, 0x43, 0x5D, 0x53, 0xCA, 0xDA,),
    (0x2C1B, 0x209, 0x403, 0x453, 0x441, 0x311, 0x15A1C, 0x354, 0x5D, 0x59, 0x4A, 0x104, 0x4B, 0xDA, 0x4D, 0xCC,),
    (0x401, 0x419, 0x49, 0x40B, 0x51, 0x113, 0x30C, 0x5B, 0x5A, 0x344, 0x314, 0x4A, 0x5C, 0x43, 0xDD, 0xCD,),
    (0x2319, 0x50B, 0x401, 0x41B, 0x451, 0x49, 0x15A, 0x1C, 0x54A, 0x104, 0x2B4C, 0x54, 0x43, 0x5D, 0xCD, 0xD3,),
    (0x401, 0x1614A, 0x314, 0x2103, 0x44D, 0x5A, 0x349, 0x519, 0x51, 0x4B, 0x304, 0x13, 0x5C, 0x5B, 0xCC, 0xDD,),
    (0x2C09, 0x4A, 0x441, 0x5D, 0x2311, 0xB, 0x43, 0x13, 0x5B, 0x1904, 0x59, 0x1C, 0x24C, 0x54, 0xDA, 0xCD,),
    (0x104, 0x50B, 0x114, 0x13, 0x443, 0x15C, 0x311, 0x54C, 0x24D, 0x5B, 0x54A, 0x259, 0x1, 0xC9, 0x5D, 0xDA,),
    (0x40B, 0x11C, 0x2319, 0x50C, 0x154, 0x5D, 0x1, 0x451, 0x1B, 0x4D, 0x44, 0x55A, 0xD3, 0x43, 0x49, 0xCA,),
    (0x413, 0x2209, 0x25B, 0x2219, 0x14, 0x51, 0x35C, 0x3, 0x14A, 0x4, 0x4B, 0x4C, 0x24D, 0xC1, 0x5D, 0xDA,),
    (0x1A09, 0x411, 0x295A, 0x1B, 0x59, 0x31C, 0xC, 0xB, 0x54, 0x344, 0x294A, 0x4D, 0x43, 0x53, 0xDD, 0xC1,),
    (0x401, 0x413, 0x411, 0x45B, 0x2259, 0x49, 0x304, 0x3, 0x34C, 0x14, 0x55C, 0x54A, 0x5A, 0xDD, 0x4D, 0xCB,),
    (0x409, 0x225D, 0x30C, 0x2A1C, 0x19, 0x51, 0x344, 0x54A, 0xB, 0x354, 0x1B, 0x53, 0x4D, 0x43, 0xC1, 0xDA,),
    (0x401, 0x4A, 0x249, 0x519, 0x304, 0x3, 0x4C, 0x4D, 0xCB, 0x14, 0x25C, 0x55A, 0x13, 0x5B, 0x5D, 0xD1,),
    (0x409, 0x44D, 0x103, 0x219, 0x4A, 0x13, 0x5A, 0x4B, 0x2351, 0x1A0C, 0x191C, 0x5B, 0x344, 0x5D, 0xD4, 0xC1,),
)

FIRST = (
    (0x288,),
    (0x1926B,),
    (0x688,),
    (0x2E9,),
    (0x688,),
    (0x253,),
    (0x8A0,),
    (0x263,),
    (0x698,),
    (0x8C9,),
    (0x288,),
    (0x6C9,),
    (0x222,),
    (0x6D92C9,),
    (0x622,),
    (0x453,),
)
FIRST_COUNT = (2, 3, 2, 2, 2, 2, 2, 2, 2, 2, 2, 2, 2, 4, 2, 2)
THEN = (
    (0x68964B, 0x0,),
    (0x22288, 0x0,),
    (0x29B2D1, 0x0,),
    (0x251288, 0x0,),
    (0x212C9A5B, 0xA,),
    (0x288, 0x0,),
    (0x9863, 0x0,),
    (0x1A898, 0x0,),
    (0xA2C9, 0x0,),
    (0x2D880A, 0x0,),
    (0x96D12E9, 0x0,),
    (0xB4D1698, 0xA,),
    (0x1B8D92C9, 0x0,),
    (0x2A0, 0x0,),
    (0x8E9, 0x0,),
    (0x186612A0, 0x1A,),
)
THEN_COUNT = (4, 3, 4, 4, 6, 2, 3, 3, 3, 4, 5, 6, 5, 2, 2, 6)

SENDS = (19, 17, 20, 18, 15, 15, 16, 13, 15, 14, 16, 17, 17, 15, 10, 19)
FAN = 3

SEEN = {
    0: ((0,), (0, 1)),
    1: ((0, 1), (0, 1)),
    2: ((1,), ()),
    3: ((0,), (0, 1)),
    4: ((0, 1), (0, 1)),
    5: ((1,), ()),
}


def pick(choices, at):
    value = jnp.int32(choices[0])
    for index in range(1, len(choices)):
        value = jnp.where(at == index, choices[index], value)
    return value


def bits(value, low, count):
    return lax.shift_right_logical(value, jnp.int32(low)) & ((1 << count) - 1)


def place(role, piece, block):
    return (role * PIECES + piece) * BLOCKS + block


def kernel(spans_ref, q_ref, k_ref, v_ref, o_ref, order_ref, held, qbuf, obuf, peak, total, acc, hidden,
           send_sem, recv_sem, swap_sem, q_sem, qswap_sem, o_sem, order_sem):
    n_outer = lax.axis_size("outer")
    n_chips = lax.axis_size("inner") // 2
    outer = lax.axis_index("outer")
    inner = lax.axis_index("inner")
    chip, core = inner // 2, inner % 2
    kind = ((outer % 2) * 4 + chip % 4) * 2 + core
    other = 1 - core

    def device(d_outer, d_chip):
        return (
            (outer + d_outer + n_outer) & (n_outer - 1),
            ((chip + d_chip + n_chips) & (n_chips - 1)) * 2 + core,
        )

    twin = (outer, chip * 2 + other)

    barrier = pltpu.get_barrier_semaphore()
    for d_outer, d_chip in OFFSETS:
        pl.semaphore_signal(barrier, 1, device_id=device(-d_outer, -d_chip), device_id_type=MESH)
    pl.semaphore_signal(barrier, 1, device_id=twin, device_id_type=MESH)

    def own_copy(ref, part, head):
        columns = pl.ds((core * HEADS + head) * HEAD, HEAD)
        return pltpu.make_async_copy(
            ref.at[:, columns], held.at[place(0, head // WIDE, core), head % WIDE, part], recv_sem.at[place(0, head // WIDE, core)]
        )

    def twin_copy(ref, part, head):
        columns = pl.ds((other * HEADS + head) * HEAD, HEAD)
        return pltpu.make_async_remote_copy(
            src_ref=ref.at[:, columns],
            dst_ref=held.at[place(0, head // WIDE, core), head % WIDE, part],
            send_sem=swap_sem.at[head, part],
            recv_sem=recv_sem.at[place(0, head // WIDE, core)],
            device_id=twin,
            device_id_type=MESH,
        )

    width = HEADS * QUARTER

    def own_queries():
        return pltpu.make_async_copy(
            q_ref.at[:, pl.ds(core * width, width)], qbuf.at[core], q_sem.at[core]
        )

    def twin_queries():
        return pltpu.make_async_remote_copy(
            src_ref=q_ref.at[:, pl.ds(other * width, width)],
            dst_ref=qbuf.at[core],
            send_sem=qswap_sem,
            recv_sem=q_sem.at[core],
            device_id=twin,
            device_id_type=MESH,
        )

    for head in range(HEADS):
        for part, ref in enumerate((k_ref, v_ref)):
            own_copy(ref, part, head).start()
    own_queries().start()
    spans = pltpu.make_async_copy(spans_ref, order_ref, order_sem)
    spans.start()

    def hidden_tile(role, query_core, key_core):
        d_outer, d_chip = role // 3, role % 3
        at_outer, at_inner = device(-d_outer, -d_chip)
        source = at_outer * (2 * n_chips) + (at_inner - core) + key_core
        mine = outer * (2 * n_chips) + chip * 2 + query_core
        row = lax.broadcasted_iota(jnp.int32, (HEAD, HEAD), 0)
        column = lax.broadcasted_iota(jnp.int32, (HEAD, HEAD), 1)
        half = HEAD // 2
        row_at = jnp.where(row < half, order_ref[2 * mine] * half, order_ref[2 * mine + 1] * half - half) + row
        column_at = (
            jnp.where(column < half, order_ref[2 * source] * half, order_ref[2 * source + 1] * half - half) + column
        )
        return jnp.where(column_at <= row_at, 0.0, MASKED)

    def copy_on(role, block, piece, there):
        far, far_there = (role + 5) >> 3, (there + 5) >> 3
        to = device(far_there - far, (there - 3 * far_there) - (role - 3 * far))
        return pltpu.make_async_remote_copy(
            src_ref=held.at[place(role, piece, block)],
            dst_ref=held.at[place(there, piece, block)],
            send_sem=send_sem,
            recv_sem=recv_sem.at[place(there, piece, block)],
            device_id=to,
            device_id_type=MESH,
        )

    def arrive(slot):
        chunk = held.at[slot]
        pltpu.make_async_copy(chunk, chunk, recv_sem.at[slot]).wait()

    def own_sends(words, count):
        @pl.loop(0, count)
        def _(step):
            code = lax.shift_right_logical(pick(words, lax.div(step, 5)), lax.rem(step, 5) * 6)
            copy_on(0, bits(code, 0, 1), bits(code, 1, 2), bits(code, 3, 3)).start()

    def column(table):
        return [pick([row[at] for row in table], kind) for at in range(len(table[0]))]

    def pass_on(code, role, block, piece, at=0):
        if at == FAN:
            return
        there = bits(code, 8 + 3 * at, 3)

        @pl.when(there > 0)
        def _():
            copy_on(role, block, piece, there).start()
            pass_on(code, role, block, piece, at + 1)

    steps = column(STEPS)
    first, then = column(FIRST), column(THEN)
    first_count, then_count = pick(FIRST_COUNT, kind), pick(THEN_COUNT, kind)
    sends = pick(SENDS, kind)

    pl.semaphore_wait(barrier, len(OFFSETS) + 1)

    for head in range(HEADS):
        for part, ref in enumerate((k_ref, v_ref)):
            twin_copy(ref, part, head).start()

    for piece in range(PIECES):
        arrive(place(0, piece, core))
    own_sends(first, first_count)
    for piece in range(PIECES):
        arrive(place(0, piece, other))
    own_sends(then, then_count)
    twin_queries().start()

    spans.wait()
    for role in range(ROLES):
        for query_core in range(2):
            for key_core in SEEN[role][query_core]:
                hidden[role, query_core, key_core] = hidden_tile(role, query_core, key_core)

    scale = math.log2(math.e) / math.sqrt(HEAD)

    def attend(seen_by, role, piece, wide, fresh=False):
        head = piece * WIDE + wide

        def gather(part, seen):
            return jnp.concatenate([held[place(role, piece, block), wide, part] for block in seen], axis=0)

        for query_core in range(2):
            seen = seen_by[query_core]
            if not seen:
                continue
            queries = jnp.concatenate(
                [
                    qbuf[query_core, :, pl.ds(pl.multiple_of((head * GROUP + at) * HEAD, HEAD), HEAD)]
                    for at in range(GROUP)
                ],
                axis=0,
            )
            score = lax.dot_general(
                queries,
                gather(0, seen),
                (((1,), (1,)), ((), ())),
                preferred_element_type=jnp.float32,
            )
            scores = [
                (
                    score[:, n * HEAD : (n + 1) * HEAD].reshape(GROUP, HEAD, HEAD) * scale
                    + hidden[role, query_core, block][None]
                ).reshape(QUARTER, HEAD)
                for n, block in enumerate(seen)
            ]
            top = scores[0] if len(seen) == 1 else jnp.maximum(scores[0], scores[1])
            top = jnp.broadcast_to(jnp.max(top, axis=1, keepdims=True), (QUARTER, HEAD))
            if not fresh:
                old = peak[query_core, head]
                top = jnp.maximum(old, top)
                factor = jnp.exp2(old - top)
            weights = [jnp.exp2(part - top) for part in scores]
            summed = weights[0] if len(seen) == 1 else weights[0] + weights[1]
            update = jnp.dot(
                jnp.concatenate([weight.astype(jnp.bfloat16) for weight in weights], axis=1),
                gather(1, seen),
                preferred_element_type=jnp.float32,
            )
            if not fresh:
                summed = total[query_core, head] * factor + summed
                update = acc[query_core, head] * factor + update
            peak[query_core, head] = top
            total[query_core, head] = summed
            acc[query_core, head] = update

    for query_core in range(2):
        pltpu.make_async_copy(qbuf.at[query_core], qbuf.at[query_core], q_sem.at[query_core]).wait()

    @pl.loop(0, HEADS)
    def _(head):
        attend(SEEN[0], 0, head // WIDE, head % WIDE, fresh=True)

    def own_result(head):
        columns = pl.ds((core * HEADS + head) * QUARTER, QUARTER)
        return pltpu.make_async_copy(obuf.at[core, head], o_ref.at[:, columns], o_sem.at[0, head])

    def twin_result(head):
        columns = pl.ds((core * HEADS + head) * QUARTER, QUARTER)
        return pltpu.make_async_remote_copy(
            src_ref=obuf.at[other, head],
            dst_ref=o_ref.at[:, columns],
            send_sem=o_sem.at[1, head],
            recv_sem=o_sem.at[2, head],
            device_id=twin,
            device_id_type=MESH,
        )

    def conclude(head):
        for query_core in range(2):
            for at in range(GROUP):
                rows = pl.ds(at * HEAD, HEAD)
                sums = jnp.sum(total[query_core, head, rows], axis=1, keepdims=True)
                result = acc[query_core, head, rows] / sums
                obuf[query_core, head, :, at * HEAD : (at + 1) * HEAD] = result.astype(jnp.bfloat16)
        twin_result(head).start()
        own_result(head).start()

    @pl.loop(0, len(steps))
    def _(step):
        code = pick(steps, step)
        role, block, piece = bits(code, 0, 3), bits(code, 3, 1), bits(code, 4, 2)
        arrive(place(role, piece, block))
        pass_on(code, role, block, piece)
        complete = bits(code, 6, 1)
        for like in (1, 2, 3):
            same = (role == like) | (role == like + 3) if like < 3 else role == 3

            @pl.when((complete == 1) & same)
            def _():
                @pl.loop(0, WIDE)
                def _(wide):
                    attend(SEEN[like], role, piece, wide)

        @pl.when(bits(code, 7, 1) == 1)
        def _():
            @pl.loop(0, WIDE)
            def _(wide):
                conclude(piece * WIDE + wide)

    for head in range(HEADS):
        for part, ref in enumerate((k_ref, v_ref)):
            twin_copy(ref, part, head).wait_send()
    twin_queries().wait_send()
    for count in sorted(set(SENDS)):
        @pl.when(sends == count)
        def _():
            sent = held.at[pl.ds(0, count)]
            pltpu.make_async_copy(sent, sent, send_sem).wait()

    @pl.loop(0, HEADS)
    def _(head):
        own_result(head).wait()
        twin_result(head).wait()


def on_device(queries, keys, values, span_order):
    rows = queries.shape[0]
    return pl.pallas_call(
        kernel,
        out_shape=jax.ShapeDtypeStruct(queries.shape, jnp.bfloat16),
        in_specs=[pl.BlockSpec(memory_space=pltpu.HBM)] * 4,
        out_specs=pl.BlockSpec(memory_space=pl.ANY),
        scratch_shapes=[
            pltpu.SMEM(span_order.shape, jnp.int32),
            pltpu.VMEM((ROLES * PIECES * BLOCKS, WIDE, 2, rows, HEAD), jnp.bfloat16),
            pltpu.VMEM((2, rows, HEADS * QUARTER), jnp.bfloat16),
            pltpu.VMEM((2, HEADS, rows, QUARTER), jnp.bfloat16),
            pltpu.VMEM((2, HEADS, QUARTER, HEAD), jnp.float32),
            pltpu.VMEM((2, HEADS, QUARTER, HEAD), jnp.float32),
            pltpu.VMEM((2, HEADS, QUARTER, HEAD), jnp.float32),
            pltpu.VMEM((ROLES, 2, 2, rows, HEAD), jnp.float32),
            pltpu.SemaphoreType.DMA,
            pltpu.SemaphoreType.DMA((ROLES * PIECES * BLOCKS,)),
            pltpu.SemaphoreType.DMA((HEADS, 2)),
            pltpu.SemaphoreType.DMA((2,)),
            pltpu.SemaphoreType.DMA,
            pltpu.SemaphoreType.DMA((3, HEADS)),
            pltpu.SemaphoreType.DMA,
        ],
        compiler_params=pltpu.CompilerParams(
            collective_id=0, has_side_effects=True, vmem_limit_bytes=52 * 2**20
        ),
        name="attend_window",
    )(*(pltpu.with_memory_space_constraint(one, pltpu.HBM) for one in (span_order, queries, keys, values)))


def solution(mesh):
    rows = P(("outer", "inner"), None)
    return jax.shard_map(
        on_device,
        mesh=mesh,
        in_specs=(rows, rows, rows, P()),
        out_specs=rows,
        check_vma=False,
    )
```

time: 58 us -> 50.9 us (0.88)
  the two profiles are of different devices: /device:TPU:25 before, /device:TPU:17 now
where the time goes in v2:
time: 50.9 us; the launch traced here: 50.8 us
  Pallas kernels  49.9 us (98%)
  local copies, waits for them, and re-layouts  0.97 us (2%)
    pallas_call x1, Pallas kernels, on_device(): pl.pallas_call(kernel, out_shape=jax.ShapeDtypeStruct(queries.shape, jnp....  49.9 us

profile of v2, /device:TPU:17, one launch (start us, length us, event | category | flops | bytes accessed | tf_op | source)
XLA Modules:
  0.0 50.8 jit_solution(9843185751816010826)
XLA Ops:
  0.0 49.9 %attend_window.1 = bf16[128,4096]{1,0:T(8,128)(2,1)S(1)} custom-call(s32[512]{0:T(512)} %spans_ref.1, bf16[128,4096]{1,0:T(8,128)(2,1)} %q_ref.1, bf16[128,1024]{1,0:T(8,128)(2,1)} %k_ref.1, bf16[128,1024]{1,0:T(8,128)(2,1)} %v_ref.1), custom_call_target="tpu_custom_call" | custom-call | tf_op jit(solution)/shard_map/attend_window/pallas_call | solution.py:373
  49.9 1.0 %copy.6 = bf16[128,4096]{1,0:T(8,128)(2,1)} copy(bf16[128,4096]{1,0:T(8,128)(2,1)S(1)} %attend_window.1) | data formatting | bytes 2097152

commit v3 on v2

--- a/solution.py
+++ b/solution.py
@@ -17,71 +17,71 @@
 MESH = pl.DeviceIdType.MESH
 MASKED = -1e30
 
-OFFSETS = ((-1, 0), (-1, 1), (-1, 2), (0, -2), (0, -1), (0, 1), (0, 2), (1, -1), (1, 0), (1, 1), (1, 2),)
+OFFSETS = ((-1, -1), (-1, 0), (-1, 1), (-1, 2), (0, -2), (0, -1), (0, 1), (0, 2), (1, -2), (1, -1), (1, 0), (1, 1), (1, 2),)
 
 WIDE = 2
 PIECES = HEADS // WIDE
 
 STEPS = (
-    (0x403, 0x114, 0x413, 0x301, 0x349, 0xC, 0x1595C, 0x311, 0x15A59, 0x44, 0x4B, 0x4A, 0x25D, 0x5B, 0xDA, 0xCD,),
-    (0x11A09, 0x2C5A, 0x104, 0x15A19, 0x441, 0x3, 0x44B, 0x4C, 0x51, 0x1B, 0x4A, 0x1C, 0x53, 0x54, 0xDD, 0xCD,),
-    (0x301, 0x411, 0x16259, 0x11A4D, 0x1B, 0x2249, 0x30C, 0x144, 0xB, 0x14, 0x2B5C, 0x43, 0x5D, 0x53, 0xCA, 0xDA,),
-    (0x2C1B, 0x209, 0x403, 0x453, 0x441, 0x311, 0x15A1C, 0x354, 0x5D, 0x59, 0x4A, 0x104, 0x4B, 0xDA, 0x4D, 0xCC,),
-    (0x401, 0x419, 0x49, 0x40B, 0x51, 0x113, 0x30C, 0x5B, 0x5A, 0x344, 0x314, 0x4A, 0x5C, 0x43, 0xDD, 0xCD,),
-    (0x2319, 0x50B, 0x401, 0x41B, 0x451, 0x49, 0x15A, 0x1C, 0x54A, 0x104, 0x2B4C, 0x54, 0x43, 0x5D, 0xCD, 0xD3,),
-    (0x401, 0x1614A, 0x314, 0x2103, 0x44D, 0x5A, 0x349, 0x519, 0x51, 0x4B, 0x304, 0x13, 0x5C, 0x5B, 0xCC, 0xDD,),
-    (0x2C09, 0x4A, 0x441, 0x5D, 0x2311, 0xB, 0x43, 0x13, 0x5B, 0x1904, 0x59, 0x1C, 0x24C, 0x54, 0xDA, 0xCD,),
-    (0x104, 0x50B, 0x114, 0x13, 0x443, 0x15C, 0x311, 0x54C, 0x24D, 0x5B, 0x54A, 0x259, 0x1, 0xC9, 0x5D, 0xDA,),
-    (0x40B, 0x11C, 0x2319, 0x50C, 0x154, 0x5D, 0x1, 0x451, 0x1B, 0x4D, 0x44, 0x55A, 0xD3, 0x43, 0x49, 0xCA,),
-    (0x413, 0x2209, 0x25B, 0x2219, 0x14, 0x51, 0x35C, 0x3, 0x14A, 0x4, 0x4B, 0x4C, 0x24D, 0xC1, 0x5D, 0xDA,),
-    (0x1A09, 0x411, 0x295A, 0x1B, 0x59, 0x31C, 0xC, 0xB, 0x54, 0x344, 0x294A, 0x4D, 0x43, 0x53, 0xDD, 0xC1,),
-    (0x401, 0x413, 0x411, 0x45B, 0x2259, 0x49, 0x304, 0x3, 0x34C, 0x14, 0x55C, 0x54A, 0x5A, 0xDD, 0x4D, 0xCB,),
-    (0x409, 0x225D, 0x30C, 0x2A1C, 0x19, 0x51, 0x344, 0x54A, 0xB, 0x354, 0x1B, 0x53, 0x4D, 0x43, 0xC1, 0xDA,),
-    (0x401, 0x4A, 0x249, 0x519, 0x304, 0x3, 0x4C, 0x4D, 0xCB, 0x14, 0x25C, 0x55A, 0x13, 0x5B, 0x5D, 0xD1,),
-    (0x409, 0x44D, 0x103, 0x219, 0x4A, 0x13, 0x5A, 0x4B, 0x2351, 0x1A0C, 0x191C, 0x5B, 0x344, 0x5D, 0xD4, 0xC1,),
+    (0x304, 0xB, 0x2301, 0x1914, 0x411, 0x43, 0x115D, 0x54C, 0x13, 0x249, 0x59, 0x55C, 0x54A, 0x5B, 0xCD, 0xDA,),
+    (0x51B, 0x1A19, 0x53, 0xC, 0x4A, 0x9, 0x441, 0xB, 0x5A, 0x43, 0x5D, 0x44, 0x51, 0xCD, 0x14, 0xDC,),
+    (0x411, 0x51B, 0x1904, 0x509, 0x53, 0x314, 0x59, 0x1615A, 0x2A4C, 0x3, 0x4D, 0x15A5C, 0x4A, 0x41, 0xCB, 0xDD,),
+    (0x2209, 0x2C0B, 0x2219, 0x214D, 0x413, 0x34A, 0x451, 0x30C, 0x41, 0x5B, 0x5A, 0x44, 0x225D, 0x4C3, 0x14, 0xDC,),
+    (0x401, 0x403, 0x2C19, 0x49, 0x51, 0x41B, 0x1C, 0x304, 0x54, 0x53, 0x2B4C, 0x4B, 0x4D, 0x5D, 0xCA, 0xDA,),
+    (0x2B09, 0x411, 0x59, 0x403, 0x441, 0x4A, 0x2B1C, 0xC, 0x4B, 0x55A, 0x154, 0x5D, 0x1B, 0x4D, 0xD3, 0xC4,),
+    (0x401, 0x14A, 0x5A, 0x19, 0x211B, 0x45D, 0x4, 0x314, 0x103, 0xAD14C, 0x53, 0x5C, 0xD1, 0x49, 0x4D, 0xCB,),
+    (0x1615A, 0x2A19, 0x351, 0x9, 0x4D, 0x15A0C, 0xB, 0x1B, 0x1A1C, 0x144, 0x43, 0x354, 0x5D, 0xD3, 0x41, 0xCA,),
+    (0x403, 0x41B, 0x4B, 0x1590C, 0x44, 0x53, 0x11, 0x309, 0x259, 0x14, 0x25D, 0x5C, 0xDA, 0x41, 0x4A, 0xCD,),
+    (0x291C, 0x224D, 0x2B19, 0x1B, 0x10C, 0x3, 0x4B, 0x2301, 0x2351, 0x5D, 0x249, 0x154, 0x4A, 0xC4, 0x53, 0xDA,),
+    (0x411, 0x413, 0x409, 0x314, 0x14A, 0x459, 0x41, 0x50B, 0x104, 0x43, 0x2A5C, 0x5D, 0x4D, 0x5B, 0xCC, 0xDA,),
+    (0x224D, 0x409, 0x3, 0x2B0C, 0x2341, 0x1C, 0x44B, 0x411, 0x459, 0x44, 0x354, 0x1B, 0x5D, 0x53, 0xCA, 0xDA,),
+    (0x401, 0x413, 0x411, 0x449, 0x59, 0xB, 0x30C, 0x344, 0x43, 0x14, 0x5B, 0x35C, 0x224D, 0x5D, 0xCA, 0xDA,),
+    (0x419, 0x41B, 0x9, 0x341, 0x403, 0x15A, 0x1C, 0x54A, 0x4D, 0x354, 0xC, 0x453, 0x4B, 0xC4, 0x5D, 0xD1,),
+    (0x113, 0x411, 0x15A, 0x25B, 0x4A, 0x1, 0x304, 0x3, 0x2B1C, 0x154, 0x114C, 0x59, 0x4D, 0xDD, 0x4B, 0xC9,),
+    (0x14A, 0x2C19, 0x5A, 0x413, 0x451, 0x103, 0x9, 0x5B, 0x35D, 0x1C, 0x4B, 0x30C, 0x144, 0x24D, 0xD4, 0xC1,),
 )
 
 FIRST = (
-    (0x288,),
-    (0x1926B,),
-    (0x688,),
-    (0x2E9,),
+    (0x298,),
+    (0x2C9,),
     (0x688,),
     (0x253,),
+    (0x688,),
+    (0x1B2E9,),
+    (0x21A,),
+    (0x8E9,),
+    (0x80A,),
+    (0x6D1253,),
+    (0x288,),
+    (0x1164B,),
+    (0x60A,),
+    (0x84B,),
     (0x8A0,),
-    (0x263,),
-    (0x698,),
-    (0x8C9,),
-    (0x288,),
-    (0x6C9,),
-    (0x222,),
-    (0x6D92C9,),
-    (0x622,),
-    (0x453,),
+    (0x2E9,),
 )
-FIRST_COUNT = (2, 3, 2, 2, 2, 2, 2, 2, 2, 2, 2, 2, 2, 4, 2, 2)
+FIRST_COUNT = (2, 2, 2, 2, 2, 3, 2, 2, 2, 4, 2, 3, 2, 2, 2, 2)
 THEN = (
-    (0x68964B, 0x0,),
-    (0x22288, 0x0,),
-    (0x29B2D1, 0x0,),
-    (0x251288, 0x0,),
-    (0x212C9A5B, 0xA,),
-    (0x288, 0x0,),
-    (0x9863, 0x0,),
-    (0x1A898, 0x0,),
-    (0xA2C9, 0x0,),
-    (0x2D880A, 0x0,),
-    (0x96D12E9, 0x0,),
-    (0xB4D1698, 0xA,),
-    (0x1B8D92C9, 0x0,),
-    (0x2A0, 0x0,),
-    (0x8E9, 0x0,),
-    (0x186612A0, 0x1A,),
+    (0x2D96C9,),
+    (0x1821B80A,),
+    (0xA4D12E1,),
+    (0x1820A,),
+    (0x2D9863,),
+    (0x960A,),
+    (0x85B,),
+    (0x61A,),
+    (0x192C9,),
+    (0x1A288,),
+    (0x1169325B,),
+    (0x1321A,),
+    (0x21B86B,),
+    (0x9298,),
+    (0x216D1,),
+    (0x19288,),
 )
-THEN_COUNT = (4, 3, 4, 4, 6, 2, 3, 3, 3, 4, 5, 6, 5, 2, 2, 6)
-
-SENDS = (19, 17, 20, 18, 15, 15, 16, 13, 15, 14, 16, 17, 17, 15, 10, 19)
-FAN = 3
+THEN_COUNT = (4, 5, 5, 3, 4, 3, 2, 2, 3, 3, 5, 3, 4, 3, 3, 3)
+
+SENDS = (18, 11, 21, 20, 14, 15, 15, 17, 13, 20, 17, 17, 15, 13, 15, 15)
+FAN = 4
 
 SEEN = {
     0: ((0,), (0, 1)),

time: 50.9 us -> 46.5 us (0.914)
  the two profiles are of different devices: /device:TPU:17 before, /device:TPU:1 now
where the time goes in v3:
time: 46.5 us; the launch traced here: 46.3 us
  Pallas kernels  45.4 us (98%)
  local copies, waits for them, and re-layouts  0.97 us (2%)
    pallas_call x1, Pallas kernels, on_device(): pl.pallas_call(kernel, out_shape=jax.ShapeDtypeStruct(queries.shape, jnp....  45.4 us
    unnamed x1, local copies, waits for them, and re-layouts  0.97 us

profile of v3, /device:TPU:1, one launch (start us, length us, event | category | flops | bytes accessed | tf_op | source)
XLA Modules:
  0.0 46.3 jit_solution(473575287659228897)
XLA Ops:
  0.0 45.4 %attend_window.1 = bf16[128,4096]{1,0:T(8,128)(2,1)S(1)} custom-call(s32[512]{0:T(512)} %spans_ref.1, bf16[128,4096]{1,0:T(8,128)(2,1)} %q_ref.1, bf16[128,1024]{1,0:T(8,128)(2,1)} %k_ref.1, bf16[128,1024]{1,0:T(8,128)(2,1)} %v_ref.1), custom_call_target="tpu_custom_call" | custom-call | tf_op jit(solution)/shard_map/attend_window/pallas_call | solution.py:373
  45.4 1.0 %copy.6 = bf16[128,4096]{1,0:T(8,128)(2,1)} copy(bf16[128,4096]{1,0:T(8,128)(2,1)S(1)} %attend_window.1) | data formatting | bytes 2097152

commit v4 on v2

--- a/solution.py
+++ b/solution.py
@@ -17,70 +17,70 @@
 MESH = pl.DeviceIdType.MESH
 MASKED = -1e30
 
-OFFSETS = ((-1, 0), (-1, 1), (-1, 2), (0, -2), (0, -1), (0, 1), (0, 2), (1, -1), (1, 0), (1, 1), (1, 2),)
+OFFSETS = ((-1, -1), (-1, 0), (-1, 1), (0, -2), (0, -1), (0, 1), (0, 2), (1, -2), (1, -1), (1, 0), (1, 1), (1, 2),)
 
 WIDE = 2
 PIECES = HEADS // WIDE
 
 STEPS = (
-    (0x403, 0x114, 0x413, 0x301, 0x349, 0xC, 0x1595C, 0x311, 0x15A59, 0x44, 0x4B, 0x4A, 0x25D, 0x5B, 0xDA, 0xCD,),
-    (0x11A09, 0x2C5A, 0x104, 0x15A19, 0x441, 0x3, 0x44B, 0x4C, 0x51, 0x1B, 0x4A, 0x1C, 0x53, 0x54, 0xDD, 0xCD,),
-    (0x301, 0x411, 0x16259, 0x11A4D, 0x1B, 0x2249, 0x30C, 0x144, 0xB, 0x14, 0x2B5C, 0x43, 0x5D, 0x53, 0xCA, 0xDA,),
-    (0x2C1B, 0x209, 0x403, 0x453, 0x441, 0x311, 0x15A1C, 0x354, 0x5D, 0x59, 0x4A, 0x104, 0x4B, 0xDA, 0x4D, 0xCC,),
-    (0x401, 0x419, 0x49, 0x40B, 0x51, 0x113, 0x30C, 0x5B, 0x5A, 0x344, 0x314, 0x4A, 0x5C, 0x43, 0xDD, 0xCD,),
-    (0x2319, 0x50B, 0x401, 0x41B, 0x451, 0x49, 0x15A, 0x1C, 0x54A, 0x104, 0x2B4C, 0x54, 0x43, 0x5D, 0xCD, 0xD3,),
-    (0x401, 0x1614A, 0x314, 0x2103, 0x44D, 0x5A, 0x349, 0x519, 0x51, 0x4B, 0x304, 0x13, 0x5C, 0x5B, 0xCC, 0xDD,),
-    (0x2C09, 0x4A, 0x441, 0x5D, 0x2311, 0xB, 0x43, 0x13, 0x5B, 0x1904, 0x59, 0x1C, 0x24C, 0x54, 0xDA, 0xCD,),
-    (0x104, 0x50B, 0x114, 0x13, 0x443, 0x15C, 0x311, 0x54C, 0x24D, 0x5B, 0x54A, 0x259, 0x1, 0xC9, 0x5D, 0xDA,),
-    (0x40B, 0x11C, 0x2319, 0x50C, 0x154, 0x5D, 0x1, 0x451, 0x1B, 0x4D, 0x44, 0x55A, 0xD3, 0x43, 0x49, 0xCA,),
-    (0x413, 0x2209, 0x25B, 0x2219, 0x14, 0x51, 0x35C, 0x3, 0x14A, 0x4, 0x4B, 0x4C, 0x24D, 0xC1, 0x5D, 0xDA,),
-    (0x1A09, 0x411, 0x295A, 0x1B, 0x59, 0x31C, 0xC, 0xB, 0x54, 0x344, 0x294A, 0x4D, 0x43, 0x53, 0xDD, 0xC1,),
-    (0x401, 0x413, 0x411, 0x45B, 0x2259, 0x49, 0x304, 0x3, 0x34C, 0x14, 0x55C, 0x54A, 0x5A, 0xDD, 0x4D, 0xCB,),
-    (0x409, 0x225D, 0x30C, 0x2A1C, 0x19, 0x51, 0x344, 0x54A, 0xB, 0x354, 0x1B, 0x53, 0x4D, 0x43, 0xC1, 0xDA,),
-    (0x401, 0x4A, 0x249, 0x519, 0x304, 0x3, 0x4C, 0x4D, 0xCB, 0x14, 0x25C, 0x55A, 0x13, 0x5B, 0x5D, 0xD1,),
-    (0x409, 0x44D, 0x103, 0x219, 0x4A, 0x13, 0x5A, 0x4B, 0x2351, 0x1A0C, 0x191C, 0x5B, 0x344, 0x5D, 0xD4, 0xC1,),
+    (0x403, 0x2301, 0x41B, 0x2311, 0x54B, 0x49, 0x53, 0x114D, 0x59, 0x14, 0x4A, 0x25D, 0x5C, 0xDA, 0xC, 0xC4,),
+    (0x50B, 0x114D, 0x413, 0x4A, 0xC, 0x411, 0x443, 0x114, 0x5A, 0x9, 0x5C, 0x341, 0x59, 0x5D, 0xC4, 0xDB,),
+    (0x403, 0x54B, 0x1, 0x11, 0x51B, 0x225D, 0x4, 0x53, 0x49, 0x4A, 0x51C, 0x44D, 0x54, 0x59, 0xDA, 0xCC,),
+    (0x224D, 0x2C0B, 0x411, 0x59, 0x194A, 0x45D, 0x15A, 0x9, 0x41, 0x2113, 0x5B, 0x15A1C, 0x1D4, 0xC, 0x44, 0xC3,),
+    (0x2113, 0x9, 0x45B, 0x19, 0x294A, 0x41, 0x104, 0x1615A, 0x51, 0x4C, 0x40B, 0x14, 0x4D, 0xC3, 0x5C, 0xDD,),
+    (0x295A, 0x19, 0x40B, 0x9, 0x51, 0x294A, 0x2143, 0x31C, 0x413, 0xC, 0x5B, 0x44D, 0x54, 0x344, 0xC1, 0xDD,),
+    (0x411, 0x401, 0x215A, 0x103, 0x2C59, 0x14, 0x44D, 0x15C, 0x11B, 0x53, 0x304, 0x4DD, 0x49, 0x4B, 0x4C, 0xCA,),
+    (0x14A, 0x45D, 0x9, 0x441, 0x11, 0x2103, 0x4D, 0x59, 0xC, 0x4B, 0x13, 0x1C, 0xC4, 0x5B, 0x54, 0xDA,),
+    (0x403, 0x413, 0x2311, 0x4B, 0x5B, 0x4, 0x24D, 0x14, 0x4C, 0x1309, 0x5C, 0x441, 0x5D, 0xCA, 0x59, 0xDA,),
+    (0x114D, 0x40B, 0x443, 0x115D, 0x1B, 0x104, 0x4C, 0x2C5A, 0x1A19, 0x4A, 0x1C, 0x54, 0x51, 0x9, 0xC1, 0xD3,),
+    (0x403, 0x411, 0x413, 0x2209, 0x224D, 0x41, 0x145D, 0x55B, 0x59, 0x4, 0x14, 0x5A, 0xDC, 0x4C, 0x4A, 0xCB,),
+    (0x419, 0x224D, 0x25D, 0x209, 0x2C1B, 0x41, 0x403, 0x453, 0x14A, 0x1C, 0x354, 0x4B, 0xC, 0xC4, 0x5A, 0xD1,),
+    (0x411, 0x59, 0x104, 0x3, 0x114, 0x9, 0x1B, 0x4A, 0x53, 0x5A, 0x44D, 0x5C, 0x4B, 0xDD, 0x4C, 0xC1,),
+    (0x40B, 0x401, 0x41B, 0x49, 0x453, 0x19, 0x4A, 0x45D, 0x1C, 0x30C, 0x4D, 0x144, 0x54, 0x51, 0xDA, 0xC3,),
+    (0x401, 0x14A, 0x10B, 0x43, 0x11B, 0x5A, 0x314, 0x4, 0x53, 0x194C, 0xA34D, 0x25C, 0x11, 0x5D, 0xD9, 0xC9,),
+    (0x15A, 0x41B, 0x19, 0x4A, 0x153, 0x44D, 0x51, 0xC, 0x9, 0x1C, 0x25D, 0xD4, 0x344, 0xB, 0x41, 0xC3,),
 )
 
 FIRST = (
+    (0x698,),
+    (0x19453,),
+    (0x698,),
+    (0x116E9,),
+    (0x20A,),
+    (0x6D9AE9,),
     (0x288,),
-    (0x1926B,),
+    (0x1BAE9,),
+    (0x298,),
+    (0x964B,),
+    (0x298,),
+    (0x1366B,),
     (0x688,),
-    (0x2E9,),
-    (0x688,),
-    (0x253,),
-    (0x8A0,),
-    (0x263,),
-    (0x698,),
-    (0x8C9,),
-    (0x288,),
-    (0x6C9,),
-    (0x222,),
-    (0x6D92C9,),
-    (0x622,),
-    (0x453,),
+    (0x194E9,),
+    (0x298,),
+    (0x2B2E9,),
 )
-FIRST_COUNT = (2, 3, 2, 2, 2, 2, 2, 2, 2, 2, 2, 2, 2, 4, 2, 2)
+FIRST_COUNT = (2, 3, 2, 3, 2, 4, 2, 3, 2, 3, 2, 3, 2, 3, 2, 3)
 THEN = (
-    (0x68964B, 0x0,),
-    (0x22288, 0x0,),
-    (0x29B2D1, 0x0,),
-    (0x251288, 0x0,),
-    (0x212C9A5B, 0xA,),
-    (0x288, 0x0,),
-    (0x9863, 0x0,),
-    (0x1A898, 0x0,),
-    (0xA2C9, 0x0,),
-    (0x2D880A, 0x0,),
-    (0x96D12E9, 0x0,),
-    (0xB4D1698, 0xA,),
-    (0x1B8D92C9, 0x0,),
-    (0x2A0, 0x0,),
-    (0x8E9, 0x0,),
-    (0x186612A0, 0x1A,),
+    (0x192884D1, 0x1B,),
+    (0x21B60A, 0x0,),
+    (0x25B4E9, 0x0,),
+    (0x28B698, 0x0,),
+    (0x1B621A4B, 0x0,),
+    (0xA688, 0x0,),
+    (0x6D9AE9, 0x0,),
+    (0x6A0, 0x0,),
+    (0x1368965B, 0x2C8,),
+    (0x861A, 0x0,),
+    (0x136916D9, 0xB,),
+    (0x251688, 0x0,),
+    (0x66BA5B, 0x0,),
+    (0xA2DB698, 0x0,),
+    (0x6E926B, 0x0,),
+    (0x699898, 0x0,),
 )
-THEN_COUNT = (4, 3, 4, 4, 6, 2, 3, 3, 3, 4, 5, 6, 5, 2, 2, 6)
-
-SENDS = (19, 17, 20, 18, 15, 15, 16, 13, 15, 14, 16, 17, 17, 15, 10, 19)
+THEN_COUNT = (6, 4, 4, 4, 5, 3, 4, 2, 7, 3, 6, 4, 4, 5, 4, 4)
+
+SENDS = (18, 15, 13, 22, 17, 18, 18, 10, 17, 17, 18, 18, 10, 15, 17, 13)
 FAN = 3
 
 SEEN = {

time: 50.9 us -> 45.9 us (0.902)
  the two profiles are of different devices: /device:TPU:17 before, /device:TPU:1 now
where the time goes in v4:
time: 45.9 us; the launch traced here: 45.4 us
  Pallas kernels  44.4 us (97%)
  local copies, waits for them, and re-layouts  0.97 us (2%)
    pallas_call x1, Pallas kernels, on_device(): pl.pallas_call(kernel, out_shape=jax.ShapeDtypeStruct(queries.shape, jnp....  44.4 us
    unnamed x1, local copies, waits for them, and re-layouts  0.97 us

profile of v4, /device:TPU:1, one launch (start us, length us, event | category | flops | bytes accessed | tf_op | source)
XLA Modules:
  0.0 45.4 jit_solution(342655209803066090)
XLA Ops:
  0.0 44.4 %attend_window.1 = bf16[128,4096]{1,0:T(8,128)(2,1)S(1)} custom-call(s32[512]{0:T(512)} %spans_ref.1, bf16[128,4096]{1,0:T(8,128)(2,1)} %q_ref.1, bf16[128,1024]{1,0:T(8,128)(2,1)} %k_ref.1, bf16[128,1024]{1,0:T(8,128)(2,1)} %v_ref.1), custom_call_target="tpu_custom_call" | custom-call | tf_op jit(solution)/shard_map/attend_window/pallas_call | solution.py:373
  44.4 1.0 %copy.6 = bf16[128,4096]{1,0:T(8,128)(2,1)} copy(bf16[128,4096]{1,0:T(8,128)(2,1)S(1)} %attend_window.1) | data formatting | bytes 2097152

commit v5 on v4

--- a/solution.py
+++ b/solution.py
@@ -23,22 +23,22 @@
 PIECES = HEADS // WIDE
 
 STEPS = (
-    (0x403, 0x2301, 0x41B, 0x2311, 0x54B, 0x49, 0x53, 0x114D, 0x59, 0x14, 0x4A, 0x25D, 0x5C, 0xDA, 0xC, 0xC4,),
-    (0x50B, 0x114D, 0x413, 0x4A, 0xC, 0x411, 0x443, 0x114, 0x5A, 0x9, 0x5C, 0x341, 0x59, 0x5D, 0xC4, 0xDB,),
-    (0x403, 0x54B, 0x1, 0x11, 0x51B, 0x225D, 0x4, 0x53, 0x49, 0x4A, 0x51C, 0x44D, 0x54, 0x59, 0xDA, 0xCC,),
-    (0x224D, 0x2C0B, 0x411, 0x59, 0x194A, 0x45D, 0x15A, 0x9, 0x41, 0x2113, 0x5B, 0x15A1C, 0x1D4, 0xC, 0x44, 0xC3,),
-    (0x2113, 0x9, 0x45B, 0x19, 0x294A, 0x41, 0x104, 0x1615A, 0x51, 0x4C, 0x40B, 0x14, 0x4D, 0xC3, 0x5C, 0xDD,),
-    (0x295A, 0x19, 0x40B, 0x9, 0x51, 0x294A, 0x2143, 0x31C, 0x413, 0xC, 0x5B, 0x44D, 0x54, 0x344, 0xC1, 0xDD,),
-    (0x411, 0x401, 0x215A, 0x103, 0x2C59, 0x14, 0x44D, 0x15C, 0x11B, 0x53, 0x304, 0x4DD, 0x49, 0x4B, 0x4C, 0xCA,),
-    (0x14A, 0x45D, 0x9, 0x441, 0x11, 0x2103, 0x4D, 0x59, 0xC, 0x4B, 0x13, 0x1C, 0xC4, 0x5B, 0x54, 0xDA,),
-    (0x403, 0x413, 0x2311, 0x4B, 0x5B, 0x4, 0x24D, 0x14, 0x4C, 0x1309, 0x5C, 0x441, 0x5D, 0xCA, 0x59, 0xDA,),
-    (0x114D, 0x40B, 0x443, 0x115D, 0x1B, 0x104, 0x4C, 0x2C5A, 0x1A19, 0x4A, 0x1C, 0x54, 0x51, 0x9, 0xC1, 0xD3,),
-    (0x403, 0x411, 0x413, 0x2209, 0x224D, 0x41, 0x145D, 0x55B, 0x59, 0x4, 0x14, 0x5A, 0xDC, 0x4C, 0x4A, 0xCB,),
-    (0x419, 0x224D, 0x25D, 0x209, 0x2C1B, 0x41, 0x403, 0x453, 0x14A, 0x1C, 0x354, 0x4B, 0xC, 0xC4, 0x5A, 0xD1,),
-    (0x411, 0x59, 0x104, 0x3, 0x114, 0x9, 0x1B, 0x4A, 0x53, 0x5A, 0x44D, 0x5C, 0x4B, 0xDD, 0x4C, 0xC1,),
-    (0x40B, 0x401, 0x41B, 0x49, 0x453, 0x19, 0x4A, 0x45D, 0x1C, 0x30C, 0x4D, 0x144, 0x54, 0x51, 0xDA, 0xC3,),
-    (0x401, 0x14A, 0x10B, 0x43, 0x11B, 0x5A, 0x314, 0x4, 0x53, 0x194C, 0xA34D, 0x25C, 0x11, 0x5D, 0xD9, 0xC9,),
-    (0x15A, 0x41B, 0x19, 0x4A, 0x153, 0x44D, 0x51, 0xC, 0x9, 0x1C, 0x25D, 0xD4, 0x344, 0xB, 0x41, 0xC3,),
+    (0x403, 0x2301, 0x41B, 0x2311, 0x54B, 0x49, 0x53, 0x114D, 0x59, 0x14, 0x25D, 0x4A, 0x5C, 0xDA, 0xC, 0xC4,),
+    (0x50B, 0x114D, 0x413, 0x4A, 0xC, 0x114, 0x443, 0x411, 0x5A, 0x5C, 0x301, 0x49, 0x59, 0x5D, 0xC4, 0xDB,),
+    (0x403, 0x54B, 0x51B, 0x1, 0x11, 0x49, 0x4A, 0x4, 0x53, 0x225D, 0x51C, 0x44D, 0x54, 0x59, 0xCC, 0xDA,),
+    (0x224D, 0x2C0B, 0x411, 0x59, 0x45D, 0x194A, 0x15A, 0x1, 0x2113, 0x49, 0x15A1C, 0x154, 0xDB, 0x4, 0x4C, 0xC3,),
+    (0x2113, 0x9, 0x45B, 0x294A, 0x19, 0x104, 0x1615A, 0x41, 0x51, 0x4C, 0x40B, 0x14, 0x4D, 0x5C, 0xDD, 0xC3,),
+    (0x295A, 0x19, 0x40B, 0x51, 0x9, 0x294A, 0x2143, 0x413, 0x31C, 0xC, 0x44D, 0x5B, 0x54, 0x344, 0xDD, 0xC1,),
+    (0x411, 0x401, 0x215A, 0x103, 0x2C59, 0x14, 0x44D, 0x15C, 0x11B, 0x45D, 0xD3, 0x4A, 0x304, 0x49, 0x4B, 0xCC,),
+    (0x14A, 0x45D, 0x401, 0x49, 0x2103, 0x11, 0x4D, 0xC, 0x4B, 0x59, 0x13, 0xC4, 0x1C, 0x54, 0x5B, 0xDA,),
+    (0x403, 0x413, 0x2311, 0x4B, 0x5B, 0x4, 0x4C, 0x24D, 0x14, 0x1309, 0x5C, 0x441, 0x5D, 0x59, 0xCA, 0xDA,),
+    (0x114D, 0x40B, 0x443, 0x115D, 0x1B, 0x104, 0x2C5A, 0x4C, 0x1A19, 0x4A, 0x1C, 0x51, 0x54, 0x9, 0xC1, 0xD3,),
+    (0x403, 0x411, 0x413, 0x2209, 0x224D, 0x41, 0x145D, 0x55B, 0x59, 0x4, 0x14, 0x4C, 0x4B, 0x5C, 0xCA, 0xDA,),
+    (0x419, 0x224D, 0x25D, 0x209, 0x2C1B, 0x41, 0x403, 0x453, 0x14A, 0x314, 0x5C, 0xC, 0x4B, 0xC4, 0x5A, 0xD1,),
+    (0x411, 0x59, 0x3, 0x104, 0x1B, 0x114, 0x9, 0x4A, 0x5A, 0x44D, 0x5C, 0x53, 0x4C, 0xDD, 0x4B, 0xC1,),
+    (0x40B, 0x401, 0x41B, 0x49, 0x453, 0x19, 0x45D, 0x30C, 0x4A, 0x4D, 0x1C, 0x144, 0x54, 0x51, 0xC3, 0xDA,),
+    (0x401, 0x14A, 0x10B, 0x5A, 0x11B, 0x43, 0x314, 0xA34D, 0x190C, 0x44, 0x53, 0x25C, 0x11, 0x59, 0xDD, 0xC9,),
+    (0x15A, 0x41B, 0x19, 0x4A, 0x153, 0x44D, 0x51, 0x9, 0xC, 0x1C, 0x25D, 0x344, 0xD4, 0xB, 0x41, 0xC3,),
 )
 
 FIRST = (

time: 45.9 us -> 45.2 us (0.985); the launches traced: 45.4 us -> 45.2 us
  no operation moved by 1% of the time
where the time goes in v5:
time: 45.2 us
  Pallas kernels  44.2 us (98%)
  local copies, waits for them, and re-layouts  0.97 us (2%)
    pallas_call x1, Pallas kernels, on_device(): pl.pallas_call(kernel, out_shape=jax.ShapeDtypeStruct(queries.shape, jnp....  44.2 us
    unnamed x1, local copies, waits for them, and re-layouts  0.97 us

profile of v5, /device:TPU:1, one launch (start us, length us, event | category | flops | bytes accessed | tf_op | source)
XLA Modules:
  0.0 45.2 jit_solution(8674461511464485725)
XLA Ops:
  0.0 44.2 %attend_window.1 = bf16[128,4096]{1,0:T(8,128)(2,1)S(1)} custom-call(s32[512]{0:T(512)} %spans_ref.1, bf16[128,4096]{1,0:T(8,128)(2,1)} %q_ref.1, bf16[128,1024]{1,0:T(8,128)(2,1)} %k_ref.1, bf16[128,1024]{1,0:T(8,128)(2,1)} %v_ref.1), custom_call_target="tpu_custom_call" | custom-call | tf_op jit(solution)/shard_map/attend_window/pallas_call | solution.py:373
  44.2 1.0 %copy.6 = bf16[128,4096]{1,0:T(8,128)(2,1)} copy(bf16[128,4096]{1,0:T(8,128)(2,1)S(1)} %attend_window.1) | data formatting | bytes 2097152
